TPU v7x, 256 devices: a whole 4x4x8 slice. The times are simulated.
256 devices in a mesh: seq: 16 (over x, y), nbr: 16 (over z, core).
Axes of the slice: x: 4, y: 4, z: 8, core: 2. Of those that a mesh axis runs over, the one named last changes fastest.
Arguments:
- tokens: bfloat16 [8192, 4096], P(('seq', 'nbr')), may hold values from -7 to 7
- nbr_embed: bfloat16 [256, 128, 896], P('seq', 'nbr'), may hold values from -7 to 7
- neighbour_table: int32 [128, 2], P('seq'), may hold values from 0 to 255, as said below
- valid_counts: int32 [128], replicated, may hold values from 1 to 2
- dec_proj: bfloat16 [4096, 3, 4096], P(None, None, 'nbr'), may hold values from -1 to 1
- enc_query: bfloat16 [896, 4096], P(None, 'nbr'), may hold values from -2 to 2
- enc_out: bfloat16 [4096, 896], P('nbr'), may hold values from -0.09375 to 0.09375
- enc_gain: float32 [896], replicated, may hold values from 0.1 to 1.9
- nbr_proj: bfloat16 [896, 2, 4096], P(None, None, 'nbr'), may hold values from -2 to 2
- out_proj: bfloat16 [4096, 4096], P('nbr'), may hold values from -0.09375 to 0.09375
Outputs:
- cross_out: bfloat16 [8192, 4096], P(('seq', 'nbr'))
- encoded: bfloat16 [32768, 896], P(('seq', 'nbr'))
Inputs may be any that keep to these rules, and one draw needn't show every extreme that they name: `neighbour_table`: for each block b of 8 groups in order, the entries of those groups are a permutation of the neighbour rows b * 16 to (b + 1) * 16 - 1.
All inputs are finite; a program needn't handle non-finite values.
Results may differ from a plain program's by a relative error of at most 0.025.
Values may be sent and summed in bfloat16 or wider, within the bound.
A program may use at most 128 MiB of HBM per device.

v0:
```python
import jax
import jax.numpy as jnp
from jax import lax
from jax.sharding import PartitionSpec as P

HEAD_DIM = 128
GROUP = 64
NLEN = 128
SEQ_LEN = 2048


def passed_along(block, axis, distance):
    devices = range(lax.axis_size(axis))
    route = [(i - distance, i) for i in devices if i - distance in devices]
    return lax.ppermute(block, axis, route)


def plain_softmax(scores):
    peak = jnp.max(scores, axis=-1, keepdims=True)
    raised = jnp.exp(scores - peak)
    return (raised / jnp.sum(raised, axis=-1, keepdims=True)).astype(jnp.bfloat16)


def masked_softmax(scores, allowed):
    live = jnp.any(allowed, axis=-1, keepdims=True)
    peak = jnp.max(jnp.where(allowed, scores, -1e30), axis=-1, keepdims=True)
    peak = jnp.where(live, peak, 0.0)
    raised = jnp.where(allowed, jnp.exp(scores - peak), 0.0)
    denominator = jnp.where(live, jnp.sum(raised, axis=-1, keepdims=True), 1.0)
    return (raised / denominator).astype(jnp.bfloat16)


def normed_rows(raw_rows, partial_sum, enc_gain):
    combined = raw_rows.astype(jnp.float32) + partial_sum
    factor = lax.rsqrt(jnp.mean(combined * combined, axis=-1, keepdims=True) + 1e-06)
    return (combined * factor * enc_gain).astype(jnp.bfloat16)


def local(
    tokens,
    nbr_embed,
    neighbour_table,
    valid_counts,
    dec_proj,
    enc_query,
    enc_out,
    enc_gain,
    nbr_proj,
    out_proj,
):
    n_nbr = lax.axis_size("nbr")
    seq_index = lax.axis_index("seq")
    member = lax.axis_index("nbr")
    model_width = tokens.shape[1]
    local_width = dec_proj.shape[2]
    head_dev = local_width // HEAD_DIM
    scale = 1.0 / HEAD_DIM**0.5
    dec_flat = dec_proj.reshape(model_width, 3 * local_width)
    projected = jnp.dot(
        lax.all_gather(tokens, "nbr", axis=0, tiled=True),
        dec_flat,
        preferred_element_type=jnp.float32,
    ).astype(jnp.bfloat16)
    tok_grp = projected.shape[0]
    ch_grp = tok_grp // GROUP
    queries = projected[:, :local_width]
    cond_key = projected[:, local_width : 2 * local_width].reshape(
        ch_grp, GROUP, head_dev, HEAD_DIM
    )
    cond_value = projected[:, 2 * local_width :].reshape(ch_grp, GROUP, head_dev, HEAD_DIM)
    grp_embed = lax.all_gather(nbr_embed, "nbr", axis=1, tiled=True)
    nb_grp = grp_embed.shape[0]
    enc_width = grp_embed.shape[2]
    row_ids = neighbour_table.reshape(-1) - seq_index * nb_grp
    ordered = jnp.take(grp_embed, row_ids, axis=0).reshape(-1, enc_width)
    enc_queries = jnp.dot(ordered, enc_query, preferred_element_type=jnp.float32).astype(
        jnp.bfloat16
    )
    enc_queries = enc_queries.reshape(ch_grp, -1, head_dev, HEAD_DIM)
    enc_scores = (
        jnp.einsum("cqhd,ckhd->chqk", enc_queries, cond_key, preferred_element_type=jnp.float32)
        * scale
    )
    enc_weights = plain_softmax(enc_scores)
    enc_att = jnp.einsum(
        "chqk,ckhd->cqhd", enc_weights, cond_value, preferred_element_type=jnp.float32
    ).astype(jnp.bfloat16)
    enc_att = enc_att.reshape(-1, local_width)
    share_rows = enc_att.shape[0] // n_nbr
    summed = lax.psum(jnp.dot(enc_att, enc_out, preferred_element_type=jnp.float32), "nbr")
    encoded_all = normed_rows(ordered, summed, enc_gain)
    encoded_mine = lax.dynamic_slice_in_dim(encoded_all, member * share_rows, share_rows, 0)
    nbr_kv = jnp.dot(
        encoded_all,
        nbr_proj.reshape(enc_width, 2 * local_width),
        preferred_element_type=jnp.float32,
    ).astype(jnp.bfloat16)
    nbr_kv = nbr_kv.reshape(ch_grp, -1, 2 * local_width)
    previous = passed_along(nbr_kv[-1], "seq", 1)
    kv_ext = jnp.concatenate([previous[None], nbr_kv], axis=0)
    key_rows = kv_ext.shape[1]
    kv_ext = kv_ext.reshape(ch_grp + 1, key_rows, 2, head_dev, HEAD_DIM)
    counts_pad = jnp.concatenate([jnp.zeros((1,), jnp.int32), valid_counts], axis=0)
    counts_ext = lax.dynamic_slice_in_dim(counts_pad, seq_index * ch_grp, ch_grp + 1, 0)
    query_pad = jnp.concatenate(
        [
            jnp.zeros((1, local_width), jnp.bfloat16),
            queries,
            jnp.zeros((GROUP - 1, local_width), jnp.bfloat16),
        ],
        axis=0,
    )
    query_pad = query_pad.reshape(ch_grp + 1, GROUP, head_dev, HEAD_DIM)
    local_ids = jnp.arange((ch_grp + 1) * GROUP, dtype=jnp.int32) - 1
    global_ids = seq_index * tok_grp + local_ids
    active = (local_ids >= 0) & (local_ids < tok_grp) & (global_ids % SEQ_LEN >= GROUP - 1)
    active = active.reshape(ch_grp + 1, GROUP)
    key_slot = jnp.arange(key_rows, dtype=jnp.int32) // NLEN
    slot_live = key_slot[None, :] < counts_ext[:, None]
    allowed = active[:, None, :, None] & slot_live[:, None, None, :]
    cca_scores = (
        jnp.einsum(
            "bqhd,bkhd->bhqk", query_pad, kv_ext[:, :, 0], preferred_element_type=jnp.float32
        )
        * scale
    )
    cca_weights = masked_softmax(cca_scores, allowed)
    cca_att = jnp.einsum(
        "bhqk,bkhd->bqhd", cca_weights, kv_ext[:, :, 1], preferred_element_type=jnp.float32
    ).astype(jnp.bfloat16)
    cca_att = cca_att.reshape(-1, local_width)[1 : tok_grp + 1]
    cross_out = lax.psum_scatter(
        jnp.dot(cca_att, out_proj, preferred_element_type=jnp.float32).astype(jnp.bfloat16),
        "nbr",
        scatter_dimension=0,
        tiled=True,
    )
    return (cross_out, encoded_mine)


def solution(mesh):
    return jax.shard_map(
        local,
        mesh=mesh,
        in_specs=(
            P(("seq", "nbr"), None),
            P("seq", "nbr", None),
            P("seq", None),
            P(),
            P(None, None, "nbr"),
            P(None, "nbr"),
            P("nbr", None),
            P(),
            P(None, None, "nbr"),
            P("nbr", None),
        ),
        out_specs=(P(("seq", "nbr"), None), P(("seq", "nbr"), None)),
        check_vma=False,
    )
```

profile of v0, /device:TPU:6, one launch (start us, length us, event | category | flops | bytes accessed | tf_op | source)
XLA Modules:
  0.0 344.8 jit_solution(4652820570967814219)
XLA Ops:
  9.6 8.8 %copy.33 = bf16[4096,3,256]{0,2,1:T(8,128)(2,1)} copy(bf16[4096,3,256]{2,0,1:T(8,128)(2,1)} %param.14) | data formatting | bytes 12582912 | tf_op args[4]
  18.5 35.8 %all-gather.3.cloned.1.call-done = bf16[16,128,896]{2,1,0:T(8,128)(2,1)} async-done(((bf16[16,8,896]{2,1,0:T(8,128)(2,1)}), bf16[16,128,896]{2,1,0:T(8,128)(2,1)}) %all-gather.3.cloned.1.call-update) | async-done | bytes 3670032 | tf_op jit(solution)/shard_map/all_gather | solution.py:71
  54.3 4.8 %gather_fusion = bf16[16,128,896]{2,1,0:T(8,128)(2,1)} fusion(bf16[16,128,896]{2,1,0:T(8,128)(2,1)} %all-gather.3.cloned.1.call-done, s32[1024]{0:T(1024)S(1)} %pad_clamp_fusion), kind=kCustom, calls=%fused_computation | custom fusion | bytes 7340096 | tf_op jit(solution)/shard_map/jit(_take)/gather | solution.py:75
  59.1 2.4 bitcast_select_fusion
  61.6 2.3 convolution_convert_fusion.2
  63.8 1.3 reshape.164
  65.2 31.5 %all-gather.5.cloned.1.call-done = bf16[512,4096]{1,0:T(8,128)(2,1)} async-done(((bf16[32,4096]{1,0:T(8,128)(2,1)}), bf16[512,4096]{1,0:T(8,128)(2,1)}) %all-gather.5.cloned.1.call-update) | async-done | bytes 4194320 | tf_op jit(solution)/shard_map/all_gather | solution.py:60
  96.7 7.5 %convolution_convert_fusion.4 = bf16[512,768]{1,0:T(8,128)(2,1)S(1)} fusion(bf16[512,4096]{1,0:T(8,128)(2,1)} %all-gather.5.cloned.1.call-done, bf16[4096,768]{0,1:T(8,128)(2,1)} %bitcast.49), kind=kOutput, calls=%fused_computation.13 | convolution fusion | flops 3221618688 | bytes 11272192 | tf_op jit(solution)/shard_map/dot_general | solution.py:59
  108.9 2.0 fusion.2
  112.0 4.3 %fusion.27 = f32[2048,896]{1,0:T(8,128)} fusion(bf16[2048,256]{0,1:T(8,128)(2,1)S(1)} %bitcast.50, bf16[256,896]{1,0:T(8,128)(2,1)S(1)} %copy-done.9), kind=kOutput, calls=%fused_computation.72 | convolution fusion | flops 939524096 | bytes 8847360 | tf_op jit(solution)/shard_map/dot_general | solution.py:90
  117.4 1.1 copy.43
  119.0 127.7 %all-reduce.2.cloned.1.call-done = f32[2048,896]{1,0:T(8,128)} async-done(((f32[2048,896]{1,0:T(8,128)}), f32[2048,896]{1,0:T(8,128)}) %all-reduce.2.cloned.1.call-update) | async-done | bytes 7340048 | tf_op jit(solution)/shard_map/psum | solution.py:90
  246.6 5.5 %multiply_reduce_fusion = f32[2048]{0:T(1024)S(1)} fusion(f32[2048,896]{1,0:T(8,128)} %all-reduce.2.cloned.1.call-done, bf16[16,128,896]{2,1,0:T(8,128)(2,1)} %gather_fusion, pred[2048]{0:T(1024)(128)(4,1)S(1)} %broadcast_bitcast_fusion), kind=kLoop, calls=%fused_computation.3 | loop fusion | flops 9172992 | bytes 11020288 | tf_op jit(solution)/shard_map/reduce_sum | solution.py:35
  252.2 1.9 copy-done.2
  254.1 1.9 multiply_convert_fusion
  256.0 2.4 convolution_convert_fusion.1
  258.4 1.3 copy-done.4
  259.7 3.4 collective-permute-start
  263.9 4.0 %concatenate.15 = bf16[8,256,2,2,128]{4,3,2,1,0:T(2,128)(2,1)} reshape(bf16[2048,512]{1,0:T(8,128)(2,1)} %copy-done.4) | data formatting | bytes 4194304 | tf_op jit(solution)/shard_map/concatenate | solution.py:100
  267.9 2.6 collective-permute-done
  270.6 2.3 copy_dynamic-update-slice_fusion
  275.0 3.2 convolution_convert_fusion
  278.2 1.6 constant_dynamic-slice_fusion
  279.8 58.4 %reduce-scatter.2.cloned.1.call-done = bf16[32,4096]{1,0:T(8,128)(2,1)} async-done(((bf16[512,4096]{1,0:T(8,128)(2,1)}), bf16[32,4096]{1,0:T(8,128)(2,1)}) %reduce-scatter.2.cloned.1.call-update) | async-done | bytes 262160 | tf_op jit(solution)/shard_map/reduce_scatter | solution.py:132
  (70 shorter events, 12.6 us)
Async XLA Ops:
  7.2 267.8 %copy-start = (bf16[256,4096]{1,0:T(8,128)(2,1)S(1)}, bf16[256,4096]{1,0:T(8,128)(2,1)}, u32[]{:S(2)}) copy-start(bf16[256,4096]{1,0:T(8,128)(2,1)} %param.19) | copy-start | bytes 6291460
  7.2 47.1 %all-gather.3.cloned.1.call-start = ((), (), s32[]{:S(2)}) async-start(), calls=%async_computation.1 | async-start | bytes 3899392 | tf_op jit(solution)/shard_map/all_gather | solution.py:71
  7.9 88.8 %all-gather.5.cloned.1.call-start = ((), (), s32[]{:S(2)}) async-start(), calls=%async_computation.2 | async-start | bytes 4456448 | tf_op jit(solution)/shard_map/all_gather | solution.py:60
  8.7 238.0 %all-reduce.2.cloned.1.call-start = ((), (), s32[]{:S(2)}) async-start(), calls=%async_computation.3 | async-start | bytes 14680064 | tf_op jit(solution)/shard_map/psum | solution.py:90
  59.1 2.4 copy-start.12
  106.6 1.0 copy-start.5
  110.9 1.0 copy-start.9
  116.3 1.2 copy-start.7
  116.3 2.3 copy-start.11
  116.3 221.9 %reduce-scatter.2.cloned.1.call-start = ((), (), s32[]{:S(2)}) async-start(), calls=%async_computation.4 | async-start | bytes 4456448 | tf_op jit(solution)/shard_map/reduce_scatter | solution.py:132
  119.0 133.2 %copy-start.10 = (f32[896]{0:T(1024)S(1)}, f32[896]{0:T(1024)}, u32[]{:S(2)}) copy-start(f32[896]{0:T(1024)} %param.17) | copy-start | bytes 10756
  246.6 5.5 %copy-start.1 = (bf16[16,128,896]{2,1,0:T(8,128)(2,1)S(1)}, bf16[16,128,896]{2,1,0:T(8,128)(2,1)}, u32[]{:S(2)}) copy-start(bf16[16,128,896]{2,1,0:T(8,128)(2,1)} %gather_fusion) | copy-start | bytes 11010052
  246.6 7.4 %copy-start.2 = (f32[2048,896]{1,0:T(8,128)S(1)}, f32[2048,896]{1,0:T(8,128)}, u32[]{:S(2)}) copy-start(f32[2048,896]{1,0:T(8,128)} %all-reduce.2.cloned.1.call-done) | copy-start | bytes 22020100
  254.1 1.9 copy-start.8
  256.0 2.4 copy-start.3
  256.0 7.6 %copy-start.6 = (bf16[512,256]{1,0:T(8,128)(2,1)S(1)}, bf16[512,256]{1,0:T(8,128)(2,1)}, u32[]{:S(2)}) copy-start(bf16[512,256]{1,0:T(8,128)(2,1)} %get-tuple-element.2) | copy-start | bytes 786436
  258.4 1.3 copy-start.4
  259.7 10.8 %collective-permute-start = (bf16[256,512]{1,0:T(8,128)(2,1)S(1)}, bf16[256,512]{1,0:T(8,128)(2,1)S(1)}, u32[]{:S(2)}, u32[]{:S(2)}) collective-permute-start(bf16[256,512]{1,0:T(8,128)(2,1)S(1)} %slice.34), channel_id=1, source_target_pairs={{0,16},{16,32},{32,48},{48,64},{64,80},{80,96},{96,112},{112,128},... | collective-permute-start | bytes 786440 | tf_op jit(solution)/shard_map/ppermute | solution.py:15
Sparse Core Ops, SparseCore 0:
  9.8 44.4 all-gather.2
  56.1 40.5 all-gather.4
  116.4 130.1 all-reduce.1
  278.3 59.8 reduce-scatter.1
where the time goes:
time: 345 us
  waiting for transfers between devices  257 us (74%)
  local copies, waits for them, and re-layouts  34 us (10%)
  matrix products  23.3 us (7%)
  between operations  14.1 us (4%)
  other arithmetic  12.2 us (4%)
  starting transfers between devices  3.72 us (1%)
    psum x1, waiting for transfers between devices, local(): lax.psum(jnp.dot(enc_att, enc_out, preferred_element_type=jnp.float32), '...  128 us
    reduce_scatter x1, waiting for transfers between devices, local(): lax.psum_scatter(jnp.dot(cca_att, out_proj, preferred_element_type=jnp.fl...  58.4 us
    all_gather x1, waiting for transfers between devices, local(): grp_embed = lax.all_gather(nbr_embed, 'nbr', axis=1, tiled=True)  35.8 us
    all_gather x1, waiting for transfers between devices, local(): lax.all_gather(tokens, 'nbr', axis=0, tiled=True)  31.5 us
    unnamed x31, local copies, waits for them, and re-layouts  15.5 us
    dot_general x1, matrix products, local(): jnp.dot(lax.all_gather(tokens, 'nbr', axis=0, tiled=True), dec_flat, pref...  7.51 us
  transfers between devices with their start and end apart: 5, of which 5 were waited for; matrix products, arithmetic and copies ran while one was open for 8% of the time, Pallas kernels for 0%

commit v1 on v0

--- a/solution.py
+++ b/solution.py
@@ -68,7 +68,8 @@
         ch_grp, GROUP, head_dev, HEAD_DIM
     )
     cond_value = projected[:, 2 * local_width :].reshape(ch_grp, GROUP, head_dev, HEAD_DIM)
-    grp_embed = lax.all_gather(nbr_embed, "nbr", axis=1, tiled=True)
+    piece_out = lax.all_to_all(jnp.stack(lax.axis_size("nbr") * [nbr_embed], 0), "nbr", 0, 0)
+    grp_embed = jnp.concatenate(piece_out, 1)
     nb_grp = grp_embed.shape[0]
     enc_width = grp_embed.shape[2]
     row_ids = neighbour_table.reshape(-1) - seq_index * nb_grp

time: 345 us -> 386 us (1.12)
  waiting for transfers between devices: 257 us -> 283 us
  starting transfers between devices: 3.72 us -> 12.4 us
  local copies, waits for them, and re-layouts: 34 us -> 41.6 us
    all_to_all x0 -> x1, waiting for transfers between devices: none -> 92.9 us  [local(): lax.all_to_all(jnp.stack(lax.axis_size('nbr') * [nbr_embed], 0), 'nbr', 0...]
    all_gather x1 -> x0, waiting for transfers between devices: 35.8 us -> none  [local(): grp_embed = lax.all_gather(nbr_embed, 'nbr', axis=1, tiled=True)]
    all_gather x1, waiting for transfers between devices: 31.5 us -> 0.02 us  [local(): lax.all_gather(tokens, 'nbr', axis=0, tiled=True)]
    all_to_all x0 -> x1, starting transfers between devices: none -> 8.75 us  [local(): lax.all_to_all(jnp.stack(lax.axis_size('nbr') * [nbr_embed], 0), 'nbr', 0...]
    all_to_all x0 -> x1, local copies, waits for them, and re-layouts: none -> 4.36 us  [local(): lax.all_to_all(jnp.stack(lax.axis_size('nbr') * [nbr_embed], 0), 'nbr', 0...]
    unnamed x31 -> x33, local copies, waits for them, and re-layouts: 15.5 us -> 15.5 us
  transfers between devices with their start and end apart: 5 -> 5, of which waited for: 5 -> 4; matrix products, arithmetic and copies ran while one was open for 8% -> 8% of each run, Pallas kernels for 0% -> 0%
where the time goes in v1:
time: 386 us
  waiting for transfers between devices  283 us (73%)
  local copies, waits for them, and re-layouts  41.6 us (11%)
  matrix products  23.3 us (6%)
  between operations  14.1 us (4%)
  starting transfers between devices  12.4 us (3%)
  other arithmetic  11.5 us (3%)
    psum x1, waiting for transfers between devices, local(): lax.psum(jnp.dot(enc_att, enc_out, preferred_element_type=jnp.float32), '...  128 us
    all_to_all x1, waiting for transfers between devices, local(): lax.all_to_all(jnp.stack(lax.axis_size('nbr') * [nbr_embed], 0), 'nbr', 0...  92.9 us
    reduce_scatter x1, waiting for transfers between devices, local(): lax.psum_scatter(jnp.dot(cca_att, out_proj, preferred_element_type=jnp.fl...  58.2 us
    unnamed x33, local copies, waits for them, and re-layouts  15.5 us
    all_to_all x1, starting transfers between devices, local(): lax.all_to_all(jnp.stack(lax.axis_size('nbr') * [nbr_embed], 0), 'nbr', 0...  8.75 us
  transfers between devices with their start and end apart: 5, of which 4 were waited for; matrix products, arithmetic and copies ran while one was open for 8% of the time, Pallas kernels for 0%

profile of v1, /device:TPU:6, one launch (start us, length us, event | category | flops | bytes accessed | tf_op | source)
XLA Modules:
  0.0 385.6 jit_solution(11231546169543000472)
XLA Ops:
  7.2 3.4 stack.2
  10.6 8.7 %all-to-all-start = ((bf16[16,16,8,896]{3,2,1,0:T(8,128)(2,1)}), bf16[16,16,8,896]{3,2,1,0:T(8,128)(2,1)}, u32[]{:S(2)}, u32[]{:S(2)}) async-start(bf16[16,16,8,896]{3,2,1,0:T(8,128)(2,1)} %stack.2), calls=%async_computation | async-start | bytes 7340032 | tf_op jit(solution)/shard_map/all_to_all | solution.py:71
  20.4 8.7 %copy.46 = bf16[4096,3,256]{0,2,1:T(8,128)(2,1)} copy(bf16[4096,3,256]{2,0,1:T(8,128)(2,1)} %param.14) | data formatting | bytes 12582912 | tf_op args[4]
  29.2 92.9 %all-to-all-done = bf16[16,16,8,896]{3,2,1,0:T(8,128)(2,1)} async-done(((bf16[16,16,8,896]{3,2,1,0:T(8,128)(2,1)}), bf16[16,16,8,896]{3,2,1,0:T(8,128)(2,1)}, u32[]{:S(2)}, u32[]{:S(2)}) %all-to-all-start) | async-done | bytes 3670048 | tf_op jit(solution)/shard_map/all_to_all | solution.py:71
  122.1 4.4 %copy.72 = bf16[16,16,8,896]{3,2,0,1:T(8,128)(2,1)} copy(bf16[16,16,8,896]{3,2,1,0:T(8,128)(2,1)} %all-to-all-done) | data formatting | bytes 7340032 | tf_op jit(solution)/shard_map/all_to_all | solution.py:71
  126.4 4.8 %gather_fusion = bf16[16,128,896]{2,1,0:T(8,128)(2,1)} fusion(bf16[16,128,896]{2,1,0:T(8,128)(2,1)} %bitcast.54, s32[1024]{0:T(1024)S(1)} %pad_clamp_fusion), kind=kCustom, calls=%fused_computation | custom fusion | bytes 7340096 | tf_op jit(solution)/shard_map/jit(_take)/gather | solution.py:76
  131.2 2.4 bitcast_select_fusion
  133.7 2.3 convolution_convert_fusion.2
  135.9 1.3 reshape.174
  137.3 7.5 %convolution_convert_fusion.4 = bf16[512,768]{1,0:T(8,128)(2,1)S(1)} fusion(bf16[512,4096]{1,0:T(8,128)(2,1)} %all-gather.2.cloned.1.call-done, bf16[4096,768]{0,1:T(8,128)(2,1)} %bitcast.55), kind=kOutput, calls=%fused_computation.14 | convolution fusion | flops 3221618688 | bytes 11272192 | tf_op jit(solution)/shard_map/dot_general | solution.py:59
  149.4 2.0 fusion.2
  152.5 4.3 %fusion.27 = f32[2048,896]{1,0:T(8,128)} fusion(bf16[2048,256]{0,1:T(8,128)(2,1)S(1)} %bitcast.56, bf16[256,896]{1,0:T(8,128)(2,1)S(1)} %copy-done.9), kind=kOutput, calls=%fused_computation.73 | convolution fusion | flops 939524096 | bytes 8847360 | tf_op jit(solution)/shard_map/dot_general | solution.py:91
  159.5 128.1 %all-reduce.2.cloned.1.call-done = f32[2048,896]{1,0:T(8,128)} async-done(((f32[2048,896]{1,0:T(8,128)}), f32[2048,896]{1,0:T(8,128)}) %all-reduce.2.cloned.1.call-update) | async-done | bytes 7340048 | tf_op jit(solution)/shard_map/psum | solution.py:91
  287.6 5.5 %multiply_reduce_fusion = f32[2048]{0:T(1024)S(1)} fusion(f32[2048,896]{1,0:T(8,128)} %all-reduce.2.cloned.1.call-done, bf16[16,128,896]{2,1,0:T(8,128)(2,1)} %gather_fusion, pred[2048]{0:T(1024)(128)(4,1)S(1)} %broadcast_bitcast_fusion), kind=kLoop, calls=%fused_computation.3 | loop fusion | flops 9172992 | bytes 11020288 | tf_op jit(solution)/shard_map/reduce_sum | solution.py:35
  293.1 1.9 copy-done.2
  295.0 1.9 multiply_convert_fusion
  297.0 2.4 convolution_convert_fusion.1
  300.7 3.4 collective-permute-start
  304.9 4.0 %concatenate.15 = bf16[8,256,2,2,128]{4,3,2,1,0:T(2,128)(2,1)} reshape(bf16[2048,512]{1,0:T(8,128)(2,1)} %copy-done.4) | data formatting | bytes 4194304 | tf_op jit(solution)/shard_map/concatenate | solution.py:101
  308.8 2.6 collective-permute-done
  311.6 2.3 copy_dynamic-update-slice_fusion
  315.9 3.3 convolution_convert_fusion
  319.2 1.6 constant_dynamic-slice_fusion
  320.8 58.2 %reduce-scatter.2.cloned.1.call-done = bf16[32,4096]{1,0:T(8,128)(2,1)} async-done(((bf16[512,4096]{1,0:T(8,128)(2,1)}), bf16[32,4096]{1,0:T(8,128)(2,1)}) %reduce-scatter.2.cloned.1.call-update) | async-done | bytes 262160 | tf_op jit(solution)/shard_map/reduce_scatter | solution.py:133
  (73 shorter events, 13.6 us)
Async XLA Ops:
  7.2 308.7 %copy-start = (bf16[256,4096]{1,0:T(8,128)(2,1)S(1)}, bf16[256,4096]{1,0:T(8,128)(2,1)}, u32[]{:S(2)}) copy-start(bf16[256,4096]{1,0:T(8,128)(2,1)} %param.19) | copy-start | bytes 6291460
  10.5 9.5 %copy-start.11 = (s32[8,2]{0,1:T(2,128)S(1)}, s32[8,2]{0,1:T(2,128)}, u32[]{:S(2)}) copy-start(s32[8,2]{0,1:T(2,128)} %param.12) | copy-start | bytes 196
  10.6 111.5 %all-to-all-start = ((bf16[16,16,8,896]{3,2,1,0:T(8,128)(2,1)}), bf16[16,16,8,896]{3,2,1,0:T(8,128)(2,1)}, u32[]{:S(2)}, u32[]{:S(2)}) async-start(bf16[16,16,8,896]{3,2,1,0:T(8,128)(2,1)} %stack.2), calls=%async_computation | async-start | bytes 7340032 | tf_op jit(solution)/shard_map/all_to_all | solution.py:71
  19.3 118.0 %all-gather.2.cloned.1.call-start = ((), (), s32[]{:S(2)}) async-start(), calls=%async_computation.2 | async-start | bytes 4456448 | tf_op jit(solution)/shard_map/all_gather | solution.py:60
  20.0 267.5 %all-reduce.2.cloned.1.call-start = ((), (), s32[]{:S(2)}) async-start(), calls=%async_computation.3 | async-start | bytes 14680064 | tf_op jit(solution)/shard_map/psum | solution.py:91
  131.2 2.4 copy-start.13
  147.2 1.0 copy-start.5
  151.5 1.0 copy-start.9
  156.8 1.2 copy-start.7
  156.8 2.3 copy-start.12
  156.8 222.3 %reduce-scatter.2.cloned.1.call-start = ((), (), s32[]{:S(2)}) async-start(), calls=%async_computation.4 | async-start | bytes 4456448 | tf_op jit(solution)/shard_map/reduce_scatter | solution.py:133
  159.5 133.6 %copy-start.10 = (f32[896]{0:T(1024)S(1)}, f32[896]{0:T(1024)}, u32[]{:S(2)}) copy-start(f32[896]{0:T(1024)} %param.17) | copy-start | bytes 10756
  287.6 5.5 %copy-start.1 = (bf16[16,128,896]{2,1,0:T(8,128)(2,1)S(1)}, bf16[16,128,896]{2,1,0:T(8,128)(2,1)}, u32[]{:S(2)}) copy-start(bf16[16,128,896]{2,1,0:T(8,128)(2,1)} %gather_fusion) | copy-start | bytes 11010052
  287.6 7.4 %copy-start.2 = (f32[2048,896]{1,0:T(8,128)S(1)}, f32[2048,896]{1,0:T(8,128)}, u32[]{:S(2)}) copy-start(f32[2048,896]{1,0:T(8,128)} %all-reduce.2.cloned.1.call-done) | copy-start | bytes 22020100
  295.0 1.9 copy-start.8
  296.9 2.4 copy-start.3
  297.0 7.6 %copy-start.6 = (bf16[512,256]{1,0:T(8,128)(2,1)S(1)}, bf16[512,256]{1,0:T(8,128)(2,1)}, u32[]{:S(2)}) copy-start(bf16[512,256]{1,0:T(8,128)(2,1)} %get-tuple-element.2) | copy-start | bytes 786436
  299.3 1.3 copy-start.4
  300.7 10.8 %collective-permute-start = (bf16[256,512]{1,0:T(8,128)(2,1)S(1)}, bf16[256,512]{1,0:T(8,128)(2,1)S(1)}, u32[]{:S(2)}, u32[]{:S(2)}) collective-permute-start(bf16[256,512]{1,0:T(8,128)(2,1)S(1)} %slice.34), channel_id=1, source_target_pairs={{0,16},{16,32},{32,48},{48,64},{64,80},{80,96},{96,112},{112,128},... | collective-permute-start | bytes 786440 | tf_op jit(solution)/shard_map/ppermute | solution.py:15
Sparse Core Ops, SparseCore 0:
  22.0 99.0 all-gather.1
  156.9 130.6 all-reduce.1
  319.3 59.7 reduce-scatter.1
